TPU v7x, 32 devices: a whole 2x2x4 slice. The times are simulated.
32 devices in a mesh: shots: 4 (over y, core), band: 8 (over z, x).
Axes of the slice: x: 2, y: 2, z: 4, core: 2. Of those that a mesh axis runs over, the one named last changes fastest.
Arguments:
- forward: bfloat16 [4, 18, 32, 32, 512], P('shots', None, None, 'band'), may hold values from -6 to 6
- adjoint: bfloat16 [4, 16, 32, 32, 512], P('shots', None, None, 'band'), may hold values from -6 to 6
- velocity: float32 [32, 32, 512], P(None, 'band'), may hold values from 1.5 to 4.5
- hessian: float32 [32, 32, 512], P('band'), may hold values from 0.1 to 2
Outputs:
- gradient: float32 [32, 32, 512], P('band', None, 'shots')
All inputs are finite; a program needn't handle non-finite values.
Results may differ from a plain program's by a relative error of at most 0.0003.
Values sent between devices are 32-bit elements; how exact they have to be, the bound alone decides.
A program may use at most 128 MiB of HBM per device.

v0:
```python
import jax
import jax.numpy as jnp
from jax import lax
from jax.sharding import PartitionSpec as P

damping = 0.05


def shards(forward, adjoint, velocity, hessian):
    stored = forward[0].astype(jnp.float32)
    acceleration = stored[2:] - 2.0 * stored[1:-1] + stored[:-2]
    correlation = jnp.sum(adjoint[0].astype(jnp.float32) * acceleration, axis=0)
    slices = adjoint.shape[1]
    partial_value = correlation * (2.0 / (slices * velocity**3))
    banded = lax.all_to_all(partial_value, "band", split_axis=0, concat_axis=1, tiled=True)
    owner_grad = lax.psum_scatter(banded, "shots", scatter_dimension=2, tiled=True)
    columns = owner_grad.shape[2]
    hess_slice = lax.dynamic_slice_in_dim(hessian, lax.axis_index("shots") * columns, columns, 2)
    owner_grad = owner_grad / (hess_slice + damping)
    return owner_grad


def solution(mesh):
    return jax.shard_map(
        shards,
        mesh=mesh,
        in_specs=(
            P("shots", None, None, "band", None),
            P("shots", None, None, "band", None),
            P(None, "band", None),
            P("band", None, None),
        ),
        out_specs=P("band", None, "shots"),
        check_vma=False,
    )
```

profile of v0, /device:TPU:0, one launch (start us, length us, event | category | flops | bytes accessed | tf_op | source)
XLA Modules:
  0.0 56.1 jit_solution(16724065922328147746)
XLA Ops:
  6.5 0.0 copy-start
  6.5 0.0 reduce-scatter.2.cloned.1.call-start
  6.5 2.5 %convert_element_type.12 = f32[1,18,32,4,512]{4,3,2,1,0:T(4,128)S(1)} convert(bf16[1,18,32,4,512]{4,3,2,1,0:T(4,128)(2,1)} %param.4) | non-fusion elementwise | flops 1179648 | bytes 7077888 | tf_op jit(solution)/shard_map/convert_element_type | solution.py:10
  9.1 0.0 copy-done
  9.1 0.0 copy-start.1
  9.1 2.5 %fusion.1 = f32[32,4,512]{2,1,0:T(4,128)S(1)} fusion(f32[1,18,32,4,512]{4,3,2,1,0:T(4,128)S(1)} %convert_element_type.12, bf16[1,16,32,4,512]{4,3,2,1,0:T(4,128)(2,1)S(1)} %copy-done), kind=kLoop, calls=%fused_computation.2 | loop fusion | flops 6225920 | bytes 14942208 | tf_op jit(solution)/shard_map/reduce_sum | solution.py:12
  11.6 0.0 copy-done.1
  11.6 0.1 divide_multiply_fusion
  11.8 16.0 %all_to_all.18 = f32[32,4,512]{2,1,0:T(4,128)S(1)} all-to-all(f32[32,4,512]{2,1,0:T(4,128)S(1)} %divide_multiply_fusion), channel_id=1, replica_groups=mesh['shots'=4,'band'=8] {'band'}, dimensions={0} | all-to-all | bytes 524288 | tf_op jit(solution)/shard_map/all_to_all | solution.py:15
  27.7 0.8 %all_to_all.16 = f32[4,32,512]{2,1,0:T(8,128)} reshape(f32[4,8,4,512]{3,2,1,0:T(4,128)S(1)} %bitcast.5) | data formatting | bytes 524288 | tf_op jit(solution)/shard_map/all_to_all | solution.py:15
  28.5 0.0 reduce-scatter.2.cloned.1.call-update
  28.6 19.2 %reduce-scatter.2.cloned.1.call-done = f32[4,32,128]{2,1,0:T(8,128)} async-done(((f32[4,32,512]{2,1,0:T(8,128)}), f32[4,32,128]{2,1,0:T(8,128)}) %reduce-scatter.2.cloned.1.call-update) | async-done | bytes 65552 | tf_op jit(solution)/shard_map/reduce_scatter | solution.py:16
  47.8 1.5 %add_divide_fusion = f32[4,32,128]{2,1,0:T(8,128)} fusion(f32[4,32,128]{2,1,0:T(8,128)} %reduce-scatter.2.cloned.1.call-done, f32[4,32,512]{2,1,0:T(8,128)} %param.7, s32[]{:T(128)S(6)} %select_n.3), kind=kLoop, calls=%fused_computation.9 | loop fusion | flops 32768 | bytes 196612 | tf_op jit(solution)/shard_map/div | solution.py:19
  (1 shorter events, 0.0 us)
Async XLA Ops:
  6.5 2.5 %copy-start = (bf16[1,16,32,4,512]{4,3,2,1,0:T(4,128)(2,1)S(1)}, bf16[1,16,32,4,512]{4,3,2,1,0:T(4,128)(2,1)}, u32[]{:S(2)}) copy-start(bf16[1,16,32,4,512]{4,3,2,1,0:T(4,128)(2,1)} %param.5) | copy-start | bytes 6291460
  6.5 41.2 %reduce-scatter.2.cloned.1.call-start = ((), (), s32[]{:S(2)}) async-start(), calls=%async_computation.2 | async-start | bytes 327680 | tf_op jit(solution)/shard_map/reduce_scatter | solution.py:16
  9.1 2.5 %copy-start.1 = (f32[32,4,512]{2,1,0:T(4,128)S(1)}, f32[32,4,512]{2,1,0:T(4,128)}, u32[]{:S(2)}) copy-start(f32[32,4,512]{2,1,0:T(4,128)} %param.6) | copy-start | bytes 786436
Sparse Core Ops, SparseCore 0:
  28.7 19.0 reduce-scatter.1
where the time goes:
time: 56.3 us; the launch traced here: 56.1 us
  waiting for transfers between devices  19.2 us (34%)
  blocking collectives  16 us (28%)
  between operations  13.4 us (24%)
  other arithmetic  6.68 us (12%)
  local copies, waits for them, and re-layouts  0.81 us (1%)
    reduce_scatter x1, waiting for transfers between devices, shards(): lax.psum_scatter(banded, 'shots', scatter_dimension=2, tiled=True)  19.2 us
    all_to_all x1, blocking collectives, shards(): lax.all_to_all(partial_value, 'band', split_axis=0, concat_axis=1, tiled=...  16 us
    reduce_sum x1, other arithmetic, shards(): correlation = jnp.sum(adjoint[0].astype(jnp.float32) * acceleration, axis=0)  2.53 us
    convert_element_type x1, other arithmetic, shards(): stored = forward[0].astype(jnp.float32)  2.52 us
    div x1, other arithmetic, shards(): owner_grad = owner_grad / (hess_slice + damping)  1.52 us
  transfers between devices with their start and end apart: 1, of which 1 were waited for; matrix products, arithmetic and copies ran while one was open for 0% of the time, Pallas kernels for 0%

commit v1 on v0

v1 whole, which is shorter than its diff:
```python
import functools

import jax
import jax.numpy as jnp
from jax import lax
from jax.experimental import pallas as pl
from jax.experimental.pallas import tpu as pltpu
from jax.sharding import PartitionSpec as P

damping = 0.05
MESH = pl.DeviceIdType.MESH


def kernel(
    S, nb, Q, L1, L2,
    f_hbm, a_hbm, v_hbm, h_hbm, out_ref,
    fbuf, abuf, vbuf, hbuf, scale, hinv, part, half, rcore, ry, own, rband,
    f_sem, a_sem, vh_sem, cs_sem, cr_sem, ys_sem, yr_sem, bs_sem, br_sem,
):
    T = a_hbm.shape[0]
    C = out_ref.shape[2]
    zb, X, _ = out_ref.shape
    xs = X // nb
    K = nb // Q
    rows = zb * S * xs
    held = zb * xs
    shots, band = lax.axis_index("shots"), lax.axis_index("band")
    core, y = shots % 2, shots // 2
    other_core = shots + 1 - 2 * core
    other_y = shots + 2 - 4 * y
    first = band // Q

    def group(k):
        return (first + k + 1) % K

    def loads(k):
        at = pl.multiple_of(group(k) * (Q * rows), Q * rows)
        return (
            pltpu.make_async_copy(f_hbm.at[:, pl.ds(at, Q * rows), :], fbuf.at[k], f_sem.at[k]),
            pltpu.make_async_copy(a_hbm.at[:, pl.ds(at, Q * rows), :], abuf.at[k], a_sem.at[k]),
        )

    for k in range(K):
        for c in loads(k):
            c.start()
    mine = pl.ds(pl.multiple_of(shots * C, C), C)
    vcopy = pltpu.make_async_copy(v_hbm.at[:, :, mine], vbuf, vh_sem.at[0])
    hcopy = pltpu.make_async_copy(h_hbm.at[:, :, mine], hbuf, vh_sem.at[1])
    vcopy.start()
    hcopy.start()

    barrier = pltpu.get_barrier_semaphore()
    pl.semaphore_signal(barrier, inc=1, device_id=(other_core, band), device_id_type=MESH)
    pl.semaphore_signal(barrier, inc=1, device_id=(other_y, band), device_id_type=MESH)
    for d in range(1, nb):
        pl.semaphore_signal(barrier, inc=1, device_id=(shots, (band + d) % nb), device_id_type=MESH)
    pl.semaphore_wait(barrier, nb + 1)

    def core_copy(k):
        return pltpu.make_async_remote_copy(
            src_ref=part.at[k, 1 - core], dst_ref=rcore.at[k],
            send_sem=cs_sem.at[k], recv_sem=cr_sem.at[k],
            device_id=(other_core, band), device_id_type=MESH)

    def y_copy(k):
        return pltpu.make_async_remote_copy(
            src_ref=half.at[k, 1 - y], dst_ref=ry.at[k],
            send_sem=ys_sem.at[k], recv_sem=yr_sem.at[k],
            device_id=(other_y, band), device_id_type=MESH)

    def band_copy(k, q, to, source, slot):
        return pltpu.make_async_remote_copy(
            src_ref=own.at[k, q], dst_ref=rband.at[source],
            send_sem=bs_sem.at[slot], recv_sem=br_sem.at[source],
            device_id=(shots, to), device_id_type=MESH)

    def compute(k):
        for c in loads(k):
            c.wait()

        def one(z, _):
            at = pl.multiple_of(z * (S * xs), S * xs)
            here = pl.ds(at, S * xs)
            q, zl = z // zb, z % zb
            f0 = fbuf[k, 0, here, :].astype(jnp.float32)
            f1 = fbuf[k, 1, here, :].astype(jnp.float32)
            d0 = f1 - f0
            acc = None
            for t in range(T):
                f2 = fbuf[k, t + 2, here, :].astype(jnp.float32)
                d1 = f2 - f1
                term = abuf[k, t, here, :].astype(jnp.float32) * (d1 - d0)
                acc = term if acc is None else acc + term
                f1, d0 = f2, d1
            return acc

        for z in range(Q * zb):
            acc = one(z, None)
            for s in range(S):
                part[k, s % 2, s // 2, z * xs:(z + 1) * xs, :] = acc[s * xs:(s + 1) * xs]
        core_copy(k).start()

    def after_core(k):
        core_copy(k).wait_recv()
        half[k] = part[k, core] + rcore[k]
        y_copy(k).start()

    def after_y(k):
        y_copy(k).wait_recv()
        g = group(k)
        for q in range(Q):
            b = g * Q + q
            lo = q * held
            at = pl.multiple_of(b * held, held)
            own[k, q] = (half[k, y, lo:lo + held, :] + ry[k, lo:lo + held, :]) * scale[pl.ds(at, held), :]

            @pl.when(b == band)
            def _():
                rband[band] = own[k, q]

            @pl.when(b != band)
            def _():
                band_copy(k, q, b, band, b).start()

    vcopy.wait()
    for z in range(v_hbm.shape[0]):
        v = vbuf[z]
        scale[z * xs:(z + 1) * xs, :] = 2.0 / (T * (v * v * v))
    hcopy.wait()
    hinv[...] = 1.0 / (hbuf[...] + damping)

    def step(i, _):
        @pl.when(i < K)
        def _():
            compute(i)

        @pl.when((i >= L1) & (i < K + L1))
        def _():
            after_core(i - L1)

        @pl.when(i >= L1 + L2)
        def _():
            after_y(i - L1 - L2)
        return 0

    lax.fori_loop(0, K + L1 + L2, step, 0)

    def put(source, _):
        @pl.when(source != band)
        def _():
            band_copy(0, 0, band, source, source).wait_recv()
        return 0

    lax.fori_loop(0, nb, put, 0)
    for source in range(nb):
        for z in range(zb):
            to = slice(source * xs, (source + 1) * xs)
            out_ref[z, to, :] = rband[source, z * xs:(z + 1) * xs, :] * hinv[z, to, :]

    def drain(k, _):
        core_copy(k).wait_send()
        y_copy(k).wait_send()
        return 0

    lax.fori_loop(0, K, drain, 0)

    def drain_band(b, _):
        @pl.when(b != band)
        def _():
            band_copy(0, 0, b, band, b).wait_send()
        return 0

    lax.fori_loop(0, nb, drain_band, 0)


def shards(S, nb, forward, adjoint, velocity, hessian):
    _, T2, Z, xs, NY = forward.shape
    T = adjoint.shape[1]
    zb, X, _ = hessian.shape
    C = NY // S
    Q = 2
    K = nb // Q
    L1, L2 = 1, 1

    def flat(a):
        a = a[0].reshape(a.shape[1], Z, xs, S, C)
        return a.transpose(0, 1, 3, 2, 4).reshape(a.shape[0], Z * S * xs, C)

    rows, held = zb * S * xs, zb * xs
    bf, f32 = jnp.bfloat16, jnp.float32
    dma = pltpu.SemaphoreType.DMA
    hbm = pl.BlockSpec(memory_space=pltpu.HBM)
    scratch = [
        pltpu.VMEM((K, T2, Q * rows, C), bf),
        pltpu.VMEM((K, T, Q * rows, C), bf),
        pltpu.VMEM((Z, xs, C), f32),
        pltpu.VMEM((zb, X, C), f32),
        pltpu.VMEM((Z * xs, C), f32),
        pltpu.VMEM((zb, X, C), f32),
        pltpu.VMEM((K, 2, 2, Q * held, C), f32),
        pltpu.VMEM((K, 2, Q * held, C), f32),
        pltpu.VMEM((K, 2, Q * held, C), f32),
        pltpu.VMEM((K, Q * held, C), f32),
        pltpu.VMEM((K, Q, held, C), f32),
        pltpu.VMEM((nb, held, C), f32),
        dma((K,)), dma((K,)), dma((2,)),
        dma((K,)), dma((K,)), dma((K,)), dma((K,)), dma((nb,)), dma((nb,)),
    ]
    return pl.pallas_call(
        functools.partial(kernel, S, nb, Q, L1, L2),
        out_shape=jax.ShapeDtypeStruct((zb, X, C), f32),
        in_specs=[hbm] * 4,
        out_specs=pl.BlockSpec(memory_space=pltpu.VMEM),
        scratch_shapes=scratch,
        compiler_params=pltpu.CompilerParams(
            collective_id=0, has_side_effects=True, vmem_limit_bytes=60 * 1024 * 1024
        ),
    )(flat(forward), flat(adjoint), velocity, hessian)


def solution(mesh):
    return jax.shard_map(
        functools.partial(shards, mesh.shape["shots"], mesh.shape["band"]),
        mesh=mesh,
        in_specs=(
            P("shots", None, None, "band", None),
            P("shots", None, None, "band", None),
            P(None, "band", None),
            P("band", None, None),
        ),
        out_specs=P("band", None, "shots"),
        check_vma=False,
    )
```

time: 56.3 us -> 18.3 us (0.33)
  waiting for transfers between devices: 19.2 us -> 0 us
  Pallas kernels: 0 us -> 16.7 us
  blocking collectives: 16 us -> 0 us
  between operations: 13.4 us -> 0.01 us
  other arithmetic: 6.68 us -> 0 us
  local copies, waits for them, and re-layouts: 0.81 us -> 1.47 us
    reduce_scatter x1 -> x0, waiting for transfers between devices: 19.2 us -> none  [shards(): lax.psum_scatter(banded, 'shots', scatter_dimension=2, tiled=True)]
    pallas_call x0 -> x1, Pallas kernels: none -> 16.7 us  [shards(): pl.pallas_call(functools.partial(kernel, S, nb, Q, L1, L2), out_shape=jax...]
    all_to_all x1 -> x0, blocking collectives: 16 us -> none  [shards(): lax.all_to_all(partial_value, 'band', split_axis=0, concat_axis=1, tiled=...]
    reduce_sum x1 -> x0, other arithmetic: 2.53 us -> none  [shards(): correlation = jnp.sum(adjoint[0].astype(jnp.float32) * acceleration, axis=0)]
    convert_element_type x1 -> x0, other arithmetic: 2.52 us -> none  [shards(): stored = forward[0].astype(jnp.float32)]
    div x1 -> x0, other arithmetic: 1.52 us -> none  [shards(): owner_grad = owner_grad / (hess_slice + damping)]
    unnamed x4 -> x1, local copies, waits for them, and re-layouts: 0.01 us -> 1.47 us
    all_to_all x2 -> x0, local copies, waits for them, and re-layouts: 0.8 us -> none  [shards(): lax.all_to_all(partial_value, 'band', split_axis=0, concat_axis=1, tiled=...]
  transfers between devices with their start and end apart: 1 -> 0, of which waited for: 1 -> 0; matrix products, arithmetic and copies ran while one was open for 0% -> 0% of each run, Pallas kernels for 0% -> 0%
where the time goes in v1:
time: 18.3 us; the launch traced here: 18.2 us
  Pallas kernels  16.7 us (91%)
  local copies, waits for them, and re-layouts  1.47 us (8%)
    pallas_call x1, Pallas kernels, shards(): pl.pallas_call(functools.partial(kernel, S, nb, Q, L1, L2), out_shape=jax...  16.7 us
    unnamed x1, local copies, waits for them, and re-layouts  1.47 us

profile of v1, /device:TPU:0, one launch (start us, length us, event | category | flops | bytes accessed | tf_op | source)
XLA Modules:
  0.0 18.2 jit_solution(6574017197616149205)
XLA Ops:
  0.0 16.7 %shard_map.46 = f32[4,32,128]{2,1,0:T(8,128)} custom-call(bf16[18,512,128]{2,1,0:T(8,128)(2,1)} %bitcast.10, bf16[16,512,128]{2,1,0:T(8,128)(2,1)} %bitcast.11, f32[32,4,512]{2,1,0:T(4,128)} %v_hbm.1, f32[4,32,512]{2,1,0:T(8,128)} %h_hbm.1), custom_call_target="tpu_custom_call" | custom-call | tf_op jit(solution)/shard_map/pallas_call | solution.py:209
  16.7 1.5 %copy.8 = f32[4,32,128]{2,1,0:T(8,128)} copy(f32[4,32,128]{2,1,0:T(8,128)} %shard_map.46) | data formatting | bytes 131072

commit v2 on v1

v2 whole, which is shorter than its diff:
```python
import functools

import jax
import jax.numpy as jnp
from jax import lax
from jax.experimental import pallas as pl
from jax.experimental.pallas import tpu as pltpu
from jax.sharding import PartitionSpec as P

damping = 0.05
MESH = pl.DeviceIdType.MESH


def kernel(
    S, nb, Q,
    f_hbm, a_hbm, v_hbm, h_hbm, out_ref,
    fbuf, abuf, vbuf, hbuf, scale, hinv, part, half, rcore, rband,
    f_sem, a_sem, vh_sem, cs_sem, cr_sem, bs_sem, br_sem,
):
    T = a_hbm.shape[0]
    C = out_ref.shape[2]
    zb, X, _ = out_ref.shape
    xs = X // nb
    K = nb // Q
    rows = zb * S * xs
    held = zb * xs
    shots, band = lax.axis_index("shots"), lax.axis_index("band")
    core, y = shots % 2, shots // 2
    other_core = shots + 1 - 2 * core
    other_y = shots + 2 - 4 * y
    first = band // Q

    def group(k):
        return (first + k + 1) % K

    def loads(k):
        at = pl.multiple_of(group(k) * (Q * rows), Q * rows)
        return (
            pltpu.make_async_copy(f_hbm.at[:, pl.ds(at, Q * rows), :], fbuf.at[k], f_sem.at[k]),
            pltpu.make_async_copy(a_hbm.at[:, pl.ds(at, Q * rows), :], abuf.at[k], a_sem.at[k]),
        )

    for k in range(K):
        for c in loads(k):
            c.start()
    mine = pl.ds(pl.multiple_of(shots * C, C), C)
    vcopies = [
        pltpu.make_async_copy(
            v_hbm.at[:, :, pl.ds(pl.multiple_of((core + 2 * i) * C, C), C)], vbuf.at[i], vh_sem.at[i + 1])
        for i in range(2)
    ]
    hcopy = pltpu.make_async_copy(h_hbm.at[:, :, mine], hbuf, vh_sem.at[0])
    for c in vcopies:
        c.start()
    hcopy.start()

    barrier = pltpu.get_barrier_semaphore()
    pl.semaphore_signal(barrier, inc=1, device_id=(other_core, band), device_id_type=MESH)
    pl.semaphore_signal(barrier, inc=1, device_id=(other_y, band), device_id_type=MESH)
    for d in range(1, nb):
        pl.semaphore_signal(barrier, inc=1, device_id=(shots, (band + d) % nb), device_id_type=MESH)
        pl.semaphore_signal(barrier, inc=1, device_id=(other_y, (band + d) % nb), device_id_type=MESH)

    def core_copy(k):
        return pltpu.make_async_remote_copy(
            src_ref=part.at[k, 1 - core], dst_ref=rcore.at[k],
            send_sem=cs_sem.at[k], recv_sem=cr_sem.at[k],
            device_id=(other_core, band), device_id_type=MESH)

    def band_copy(k, q, toy, to, sy, source):
        return pltpu.make_async_remote_copy(
            src_ref=half.at[k, toy, q], dst_ref=rband.at[sy, source],
            send_sem=bs_sem.at[toy, to], recv_sem=br_sem.at[sy, source],
            device_id=(core + 2 * toy, to), device_id_type=MESH)

    def compute(k):
        for c in loads(k):
            c.wait()

        def one(z, _):
            at = pl.multiple_of(z * (S * xs), S * xs)
            here = pl.ds(at, S * xs)
            q, zl = z // zb, z % zb
            f0 = fbuf[k, 0, here, :].astype(jnp.float32)
            f1 = fbuf[k, 1, here, :].astype(jnp.float32)
            d0 = f1 - f0
            acc = None
            for t in range(T):
                f2 = fbuf[k, t + 2, here, :].astype(jnp.float32)
                d1 = f2 - f1
                term = abuf[k, t, here, :].astype(jnp.float32) * (d1 - d0)
                acc = term if acc is None else acc + term
                f1, d0 = f2, d1
            return acc

        for z in range(Q * zb):
            acc = one(z, None)
            for s in range(S):
                part[k, s % 2, s // 2, z * xs:(z + 1) * xs, :] = acc[s * xs:(s + 1) * xs]

    def after_core(k):
        core_copy(k).wait_recv()
        g = group(k)
        for q in range(Q):
            b = g * Q + q
            lo = q * held
            at = pl.multiple_of(b * held, held)
            for toy in range(2):
                half[k, toy, q] = (
                    part[k, core, toy, lo:lo + held, :] + rcore[k, toy, lo:lo + held, :]
                ) * scale[toy, pl.ds(at, held), :]
        for q in range(Q):
            b = g * Q + q
            for toy in range(2):
                @pl.when((b == band) & (toy == y))
                def _():
                    rband[y, band] = half[k, toy, q]

                @pl.when((b != band) | (toy != y))
                def _():
                    band_copy(k, q, toy, b, y, band).start()

    for i in range(2):
        vcopies[i].wait()
        for z in range(v_hbm.shape[0]):
            v = vbuf[i, z]
            scale[i, z * xs:(z + 1) * xs, :] = 2.0 / (T * (v * v * v))
    hcopy.wait()
    hinv[...] = 1.0 / (hbuf[...] + damping)

    def work(k, _):
        compute(k)
        return 0

    lax.fori_loop(0, K, work, 0)
    pl.semaphore_wait(barrier, 2 * nb)

    def send(k, _):
        core_copy(k).start()
        return 0

    lax.fori_loop(0, K, send, 0)

    def step(k, _):
        after_core(k)
        return 0

    lax.fori_loop(0, K, step, 0)

    def put(source, _):
        for sy in range(2):
            @pl.when((source != band) | (sy != y))
            def _():
                band_copy(0, 0, sy, source, sy, source).wait_recv()
        return 0

    lax.fori_loop(0, nb, put, 0)
    for source in range(nb):
        for z in range(zb):
            to = slice(source * xs, (source + 1) * xs)
            rows_z = slice(z * xs, (z + 1) * xs)
            out_ref[z, to, :] = (rband[0, source, rows_z, :] + rband[1, source, rows_z, :]) * hinv[z, to, :]

    def drain(k, _):
        core_copy(k).wait_send()
        return 0

    lax.fori_loop(0, K, drain, 0)

    def drain_band(b, _):
        for toy in range(2):
            @pl.when((b != band) | (toy != y))
            def _():
                band_copy(0, 0, toy, b, y, band).wait_send()
        return 0

    lax.fori_loop(0, nb, drain_band, 0)


def shards(S, nb, forward, adjoint, velocity, hessian):
    _, T2, Z, xs, NY = forward.shape
    T = adjoint.shape[1]
    zb, X, _ = hessian.shape
    C = NY // S
    Q = 4
    K = nb // Q

    def flat(a):
        a = a[0].reshape(a.shape[1], Z, xs, S, C)
        return a.transpose(0, 1, 3, 2, 4).reshape(a.shape[0], Z * S * xs, C)

    rows, held = zb * S * xs, zb * xs
    bf, f32 = jnp.bfloat16, jnp.float32
    dma = pltpu.SemaphoreType.DMA
    hbm = pl.BlockSpec(memory_space=pltpu.HBM)
    scratch = [
        pltpu.VMEM((K, T2, Q * rows, C), bf),
        pltpu.VMEM((K, T, Q * rows, C), bf),
        pltpu.VMEM((2, Z, xs, C), f32),
        pltpu.VMEM((zb, X, C), f32),
        pltpu.VMEM((2, Z * xs, C), f32),
        pltpu.VMEM((zb, X, C), f32),
        pltpu.VMEM((K, 2, 2, Q * held, C), f32),
        pltpu.VMEM((K, 2, Q, held, C), f32),
        pltpu.VMEM((K, 2, Q * held, C), f32),
        pltpu.VMEM((2, nb, held, C), f32),
        dma((K,)), dma((K,)), dma((3,)),
        dma((K,)), dma((K,)), dma((2, nb)), dma((2, nb)),
    ]
    return pl.pallas_call(
        functools.partial(kernel, S, nb, Q),
        out_shape=jax.ShapeDtypeStruct((zb, X, C), f32),
        in_specs=[hbm] * 4,
        out_specs=pl.BlockSpec(memory_space=pltpu.VMEM),
        scratch_shapes=scratch,
        compiler_params=pltpu.CompilerParams(
            collective_id=0, has_side_effects=True, vmem_limit_bytes=60 * 1024 * 1024
        ),
    )(flat(forward), flat(adjoint), velocity, hessian)


def solution(mesh):
    return jax.shard_map(
        functools.partial(shards, mesh.shape["shots"], mesh.shape["band"]),
        mesh=mesh,
        in_specs=(
            P("shots", None, None, "band", None),
            P("shots", None, None, "band", None),
            P(None, "band", None),
            P("band", None, None),
        ),
        out_specs=P("band", None, "shots"),
        check_vma=False,
    )
```

time: 18.3 us -> 15.2 us (0.83)
  Pallas kernels: 16.7 us -> 13.6 us
    pallas_call x1, Pallas kernels: 16.7 us -> 13.6 us  [shards(): pl.pallas_call(functools.partial(kernel, S, nb, Q), out_shape=jax.ShapeDt...]
where the time goes in v2:
time: 15.2 us; the launch traced here: 15.1 us
  Pallas kernels  13.6 us (89%)
  local copies, waits for them, and re-layouts  1.47 us (10%)
    pallas_call x1, Pallas kernels, shards(): pl.pallas_call(functools.partial(kernel, S, nb, Q), out_shape=jax.ShapeDt...  13.6 us
    unnamed x1, local copies, waits for them, and re-layouts  1.47 us

profile of v2, /device:TPU:0, one launch (start us, length us, event | category | flops | bytes accessed | tf_op | source)
XLA Modules:
  0.0 15.1 jit_solution(2475937010250995926)
XLA Ops:
  0.0 13.6 %shard_map.46 = f32[4,32,128]{2,1,0:T(8,128)} custom-call(bf16[18,512,128]{2,1,0:T(8,128)(2,1)} %bitcast.10, bf16[16,512,128]{2,1,0:T(8,128)(2,1)} %bitcast.11, f32[32,4,512]{2,1,0:T(4,128)} %v_hbm.1, f32[4,32,512]{2,1,0:T(8,128)} %h_hbm.1), custom_call_target="tpu_custom_call" | custom-call | tf_op jit(solution)/shard_map/pallas_call | solution.py:210
  13.6 1.5 %copy.8 = f32[4,32,128]{2,1,0:T(8,128)} copy(f32[4,32,128]{2,1,0:T(8,128)} %shard_map.46) | data formatting | bytes 131072

commit v3 on v2

--- a/solution.py
+++ b/solution.py
@@ -40,9 +40,8 @@
             pltpu.make_async_copy(a_hbm.at[:, pl.ds(at, Q * rows), :], abuf.at[k], a_sem.at[k]),
         )
 
-    for k in range(K):
-        for c in loads(k):
-            c.start()
+    for c in loads(0):
+        c.start()
     mine = pl.ds(pl.multiple_of(shots * C, C), C)
     vcopies = [
         pltpu.make_async_copy(
@@ -52,6 +51,9 @@
     hcopy = pltpu.make_async_copy(h_hbm.at[:, :, mine], hbuf, vh_sem.at[0])
     for c in vcopies:
         c.start()
+    for k in range(1, K):
+        for c in loads(k):
+            c.start()
     hcopy.start()
 
     barrier = pltpu.get_barrier_semaphore()
@@ -120,32 +122,34 @@
                 def _():
                     band_copy(k, q, toy, b, y, band).start()
 
+    for k in range(1):
+        compute(k)
+    pl.semaphore_wait(barrier, 2 * nb)
+    for k in range(1):
+        core_copy(k).start()
+
     for i in range(2):
         vcopies[i].wait()
         for z in range(v_hbm.shape[0]):
             v = vbuf[i, z]
             scale[i, z * xs:(z + 1) * xs, :] = 2.0 / (T * (v * v * v))
+
+    def step(k, _):
+        compute(k)
+        core_copy(k).start()
+        after_core(k - 1)
+        return 0
+
+    lax.fori_loop(1, K, step, 0)
+
+    def tail(k, _):
+        after_core(k)
+        return 0
+
+    lax.fori_loop(K - 1, K, tail, 0)
+
     hcopy.wait()
     hinv[...] = 1.0 / (hbuf[...] + damping)
-
-    def work(k, _):
-        compute(k)
-        return 0
-
-    lax.fori_loop(0, K, work, 0)
-    pl.semaphore_wait(barrier, 2 * nb)
-
-    def send(k, _):
-        core_copy(k).start()
-        return 0
-
-    lax.fori_loop(0, K, send, 0)
-
-    def step(k, _):
-        after_core(k)
-        return 0
-
-    lax.fori_loop(0, K, step, 0)
 
     def put(source, _):
         for sy in range(2):

time: 15.2 us -> 14.3 us (0.941)
  Pallas kernels: 13.6 us -> 12.7 us
    pallas_call x1, Pallas kernels: 13.6 us -> 12.7 us  [shards(): pl.pallas_call(functools.partial(kernel, S, nb, Q), out_shape=jax.ShapeDt...]
where the time goes in v3:
time: 14.3 us; the launch traced here: 14.1 us
  Pallas kernels  12.7 us (89%)
  local copies, waits for them, and re-layouts  1.47 us (10%)
    pallas_call x1, Pallas kernels, shards(): pl.pallas_call(functools.partial(kernel, S, nb, Q), out_shape=jax.ShapeDt...  12.7 us
    unnamed x1, local copies, waits for them, and re-layouts  1.47 us

profile of v3, /device:TPU:0, one launch (start us, length us, event | category | flops | bytes accessed | tf_op | source)
XLA Modules:
  0.0 14.1 jit_solution(12150034358563468401)
XLA Ops:
  0.0 12.7 %shard_map.46 = f32[4,32,128]{2,1,0:T(8,128)} custom-call(bf16[18,512,128]{2,1,0:T(8,128)(2,1)} %bitcast.10, bf16[16,512,128]{2,1,0:T(8,128)(2,1)} %bitcast.11, f32[32,4,512]{2,1,0:T(4,128)} %v_hbm.1, f32[4,32,512]{2,1,0:T(8,128)} %h_hbm.1), custom_call_target="tpu_custom_call" | custom-call | tf_op jit(solution)/shard_map/pallas_call | solution.py:214
  12.7 1.5 %copy.8 = f32[4,32,128]{2,1,0:T(8,128)} copy(f32[4,32,128]{2,1,0:T(8,128)} %shard_map.46) | data formatting | bytes 131072

commit v4 on v3

--- a/solution.py
+++ b/solution.py
@@ -218,7 +218,7 @@
         out_specs=pl.BlockSpec(memory_space=pltpu.VMEM),
         scratch_shapes=scratch,
         compiler_params=pltpu.CompilerParams(
-            collective_id=0, has_side_effects=True, vmem_limit_bytes=60 * 1024 * 1024
+            collective_id=0, has_side_effects=True, vmem_limit_bytes=56360960
         ),
     )(flat(forward), flat(adjoint), velocity, hessian)
 

time: 14.3 us -> 12.8 us (0.90)
  local copies, waits for them, and re-layouts: 1.47 us -> 0.63 us
  Pallas kernels: 12.7 us -> 12 us
    unnamed x1, local copies, waits for them, and re-layouts: 1.47 us -> 0.63 us
    pallas_call x1, Pallas kernels: 12.7 us -> 12 us  [shards(): pl.pallas_call(functools.partial(kernel, S, nb, Q), out_shape=jax.ShapeDt...]
where the time goes in v4:
time: 12.8 us; the launch traced here: 12.7 us
  Pallas kernels  12 us (94%)
  local copies, waits for them, and re-layouts  0.63 us (5%)
    pallas_call x1, Pallas kernels, shards(): pl.pallas_call(functools.partial(kernel, S, nb, Q), out_shape=jax.ShapeDt...  12 us
    unnamed x1, local copies, waits for them, and re-layouts  0.63 us

profile of v4, /device:TPU:0, one launch (start us, length us, event | category | flops | bytes accessed | tf_op | source)
XLA Modules:
  0.0 12.7 jit_solution(7268507299691109643)
XLA Ops:
  0.0 12.0 %shard_map.46 = f32[4,32,128]{2,1,0:T(8,128)S(1)} custom-call(bf16[18,512,128]{2,1,0:T(8,128)(2,1)} %bitcast.10, bf16[16,512,128]{2,1,0:T(8,128)(2,1)} %bitcast.11, f32[32,4,512]{2,1,0:T(4,128)} %v_hbm.1, f32[4,32,512]{2,1,0:T(8,128)} %h_hbm.1), custom_call_target="tpu_custom_call" | custom-call | tf_op jit(solution)/shard_map/pallas_call | solution.py:214
  12.0 0.6 %copy.8 = f32[4,32,128]{2,1,0:T(8,128)} copy(f32[4,32,128]{2,1,0:T(8,128)S(1)} %shard_map.46) | data formatting | bytes 131072
